TPU v7x, 32 devices: a whole 2x2x4 slice. The times are simulated.
32 devices in a mesh: seq: 4 (over z), exp: 4 (over y, x), edp: 2 (over core).
Axes of the slice: x: 2, y: 2, z: 4, core: 2. Of those that a mesh axis runs over, the one named last changes fastest.
Arguments:
- tokens: bfloat16 [4096, 2048], P(('seq', 'exp', 'edp')), may hold values from -6 to 6
- route_ids: int32 [4096, 8], P(('seq', 'exp', 'edp')), may hold values from 0 to 15, all different within a row; in each aligned block of 128 rows (0 to 127, 128 to 255, ...) at most 72 rows name the same one
- gates: float32 [4096, 8], P(('seq', 'exp', 'edp')), may hold values from 0.05 to 0.5
- d_out: bfloat16 [4096, 2048], P(('seq', 'exp', 'edp')), may hold values from -6 to 6
- w_gate: bfloat16 [16, 2048, 384], P(('seq', 'exp')), may hold values from -0.125 to 0.125
- w_up: bfloat16 [16, 2048, 384], P(('seq', 'exp')), may hold values from -0.125 to 0.125
- w_down: bfloat16 [16, 2048, 384], P(('seq', 'exp')), may hold values from -0.3125 to 0.3125
Outputs:
- d_tokens: bfloat16 [4096, 2048], P(('seq', 'exp', 'edp'))
- grad_gate: float32 [16, 2048, 384], P(('seq', 'exp'), 'edp')
- grad_up: float32 [16, 2048, 384], P(('seq', 'exp'), 'edp')
- grad_down: float32 [16, 2048, 384], P(('seq', 'exp'), 'edp')
Inputs may be any that keep to these rules, and one draw needn't show every extreme that they name: `route_ids`: among the 128 tokens of one device no expert is named more than 72 times, a bound that some block reaches; a token names 8 different experts.
All inputs are finite; a program needn't handle non-finite values.
Results may differ from a plain program's by a relative error of at most 0.0064.
Values may be sent and summed in bfloat16 or wider, within the bound.
A program may use at most 128 MiB of HBM per device.

v0:
```python
import jax
import jax.numpy as jnp
from jax import lax
from jax.sharding import PartitionSpec as P


def expert_grads(x_rows, dy_rows, wg, wu, wd):
    a = jnp.dot(x_rows, wg, preferred_element_type=jnp.float32)
    b = jnp.dot(x_rows, wu, preferred_element_type=jnp.float32)
    sig = jax.nn.sigmoid(a)
    act = a * sig
    hidden = (act * b).astype(jnp.bfloat16)
    d_hidden = jnp.dot(dy_rows, wd, preferred_element_type=jnp.float32)
    d_gate = (d_hidden * b * sig * (1.0 + a * (1.0 - sig))).astype(jnp.bfloat16)
    d_upper = (d_hidden * act).astype(jnp.bfloat16)
    contract_one = (((1,), (1,)), ((), ()))
    contract_zero = (((0,), (0,)), ((), ()))
    back = lax.dot_general(d_gate, wg, contract_one, preferred_element_type=jnp.float32)
    back = back + lax.dot_general(d_upper, wu, contract_one, preferred_element_type=jnp.float32)
    grad_g = lax.dot_general(x_rows, d_gate, contract_zero, preferred_element_type=jnp.float32)
    grad_u = lax.dot_general(x_rows, d_upper, contract_zero, preferred_element_type=jnp.float32)
    grad_d = lax.dot_general(dy_rows, hidden, contract_zero, preferred_element_type=jnp.float32)
    return (back.astype(jnp.bfloat16), grad_g, grad_u, grad_d)


def on_device(tokens, route_ids, gates, d_out, w_gate, w_up, w_down):
    tok_count = tokens.shape[0]
    width = tokens.shape[1]
    topk = route_ids.shape[1]
    seq_count = lax.axis_size("seq")
    exp_count = lax.axis_size("exp")
    experts = seq_count * exp_count
    pairs = tok_count * topk
    capacity = pairs // experts + max(1, pairs // (8 * experts))
    flat_ids = route_ids.reshape(-1)
    onehot = (flat_ids[:, None] == jnp.arange(experts, dtype=jnp.int32)[None, :]).astype(jnp.int32)
    earlier = jnp.cumsum(onehot, axis=0) - onehot
    slot_index = jnp.sum(earlier * onehot, axis=1)
    target = flat_ids * capacity + slot_index
    rows_x = jnp.broadcast_to(tokens[:, None, :], (tok_count, topk, width)).reshape(pairs, width)
    scaled = (
        (gates[:, :, None] * d_out[:, None, :].astype(jnp.float32))
        .astype(jnp.bfloat16)
        .reshape(pairs, width)
    )
    send_x = jnp.zeros((experts * capacity, width), jnp.bfloat16).at[target].set(rows_x)
    send_dy = jnp.zeros((experts * capacity, width), jnp.bfloat16).at[target].set(scaled)
    shaped = (experts, capacity, width)
    recv_x, recv_dy = (
        lax.all_to_all(
            send_x.reshape(shaped), ("seq", "exp"), split_axis=0, concat_axis=0, tiled=True
        ),
        lax.all_to_all(
            send_dy.reshape(shaped), ("seq", "exp"), split_axis=0, concat_axis=0, tiled=True
        ),
    )
    back, grad_g, grad_u, grad_d = expert_grads(
        recv_x.reshape(experts * capacity, width),
        recv_dy.reshape(experts * capacity, width),
        w_gate[0],
        w_up[0],
        w_down[0],
    )
    returned = lax.all_to_all(
        back.reshape(experts, capacity, width),
        ("seq", "exp"),
        split_axis=0,
        concat_axis=0,
        tiled=True,
    )
    returned = returned.reshape(experts * capacity, width)
    gathered = returned[target].reshape(tok_count, topk, width).astype(jnp.float32)
    d_tokens = jnp.sum(gathered, axis=1).astype(jnp.bfloat16)
    sum_g, sum_u, sum_d = (
        lax.psum_scatter(grad_g, "edp", scatter_dimension=0, tiled=True),
        lax.psum_scatter(grad_u, "edp", scatter_dimension=0, tiled=True),
        lax.psum_scatter(grad_d, "edp", scatter_dimension=0, tiled=True),
    )
    return (d_tokens, sum_g[None], sum_u[None], sum_d[None])


def solution(mesh):
    in_specs = (
        P(("seq", "exp", "edp"), None),
        P(("seq", "exp", "edp"), None),
        P(("seq", "exp", "edp"), None),
        P(("seq", "exp", "edp"), None),
        P(("seq", "exp"), None, None),
        P(("seq", "exp"), None, None),
        P(("seq", "exp"), None, None),
    )
    out_specs = (
        P(("seq", "exp", "edp"), None),
        P(("seq", "exp"), "edp", None),
        P(("seq", "exp"), "edp", None),
        P(("seq", "exp"), "edp", None),
    )
    return jax.shard_map(
        on_device, mesh=mesh, in_specs=in_specs, out_specs=out_specs, check_vma=False
    )
```

profile of v0, /device:TPU:14, one launch (start us, length us, event | category | flops | bytes accessed | tf_op | source)
XLA Modules:
  0.0 413.5 jit_solution(11042983863596940663)
XLA Ops:
  7.2 0.0 copy-start
  7.2 0.8 broadcast_multiply_fusion
  8.0 0.8 copy.14
  8.8 0.1 eq.29
  8.9 0.1 eq.25
  9.0 0.1 copy.13
  9.1 0.1 mul.60
  9.2 4.5 %reduce-window.6 = s32[16,8,128]{2,1,0:T(8,128)S(1)} reduce-window(s32[16,8,128]{2,1,0:T(8,128)S(1)} %fusion.26, s32[]{:T(128)} %constant.7.clone.1), window={size=1x1x128 pad=0_0x0_0x127_0}, to_apply=%region_0.0 | reduce-window | flops 2080768 | bytes 131076 | tf_op jit(solution)/shard_map/reduce-window
  13.7 0.1 slice.10
  13.8 0.1 copy.16
  13.9 0.1 copy.17
  14.0 0.1 broadcast_add_fusion
  14.2 9.8 %scatter_custom_fusion.1 = bf16[1152,2048]{1,0:T(8,128)(2,1)} fusion(s32[1024]{0:T(1024)S(1)} %bitcast.72, bf16[]{:T(256)} %constant.5.clone.1, bf16[128,2048]{1,0:T(8,128)(2,1)} %param.7), kind=kCustom, calls=%fused_computation.9 | custom fusion | bytes 5242882 | tf_op jit(solution)/shard_map/scatter | solution.py:46
  24.0 0.0 copy-start.7
  24.0 0.0 copy-start.6
  24.0 7.3 %all-to-all-start.1 = ((bf16[16,72,2048]{2,1,0:T(8,128)(2,1)}), bf16[16,72,2048]{2,1,0:T(8,128)(2,1)}, u32[]{:S(2)}, u32[]{:S(2)}) async-start(bf16[16,72,2048]{2,1,0:T(8,128)(2,1)} %bitcast.67), calls=%async_computation.1 | async-start | bytes 9437184 | tf_op jit(solution)/shard_map/all_to_all | solution.py:50
  31.2 0.0 copy-done.7
  31.3 0.1 copy.18
  31.4 0.1 mul.62
  31.4 0.0 copy-done.6
  31.5 0.1 convert_element_type.31
  31.6 9.8 %scatter_custom_fusion = bf16[1152,2048]{1,0:T(8,128)(2,1)} fusion(s32[1024]{0:T(1024)S(1)} %bitcast.73, f32[128,2048]{1,0:T(8,128)S(1)} %convert_element_type.31, f32[1024]{0:T(1024)S(1)} %mul.62, bf16[]{:T(256)} %constant.5.clone.1), kind=kCustom, calls=%fused_computation.7 | custom fusion | flops 4194304 | bytes 5771266 | tf_op jit(solution)/shard_map/scatter | solution.py:47
  41.4 96.4 %all-to-all-done.1 = bf16[16,72,2048]{2,1,0:T(8,128)(2,1)} async-done(((bf16[16,72,2048]{2,1,0:T(8,128)(2,1)}), bf16[16,72,2048]{2,1,0:T(8,128)(2,1)}, u32[]{:S(2)}, u32[]{:S(2)}) %all-to-all-start.1) | async-done | bytes 4718624 | tf_op jit(solution)/shard_map/all_to_all | solution.py:50
  137.8 5.1 %all-to-all-start = ((bf16[16,72,2048]{2,1,0:T(8,128)(2,1)}), bf16[16,72,2048]{2,1,0:T(8,128)(2,1)}, u32[]{:S(2)}, u32[]{:S(2)}) async-start(bf16[16,72,2048]{2,1,0:T(8,128)(2,1)} %bitcast.66), calls=%async_computation | async-start | bytes 9437184 | tf_op jit(solution)/shard_map/all_to_all | solution.py:53
  142.9 0.0 reduce-scatter.8.cloned.1.call-start
  143.0 0.0 copy-done
  143.0 0.0 copy-start.2
  143.0 6.3 %fusion.14 = f32[1152,384]{1,0:T(8,128)} fusion(bf16[1152,2048]{1,0:T(8,128)(2,1)} %bitcast.10, bf16[1,2048,384]{2,1,0:T(8,128)(2,1)S(1)} %copy-done), kind=kOutput, calls=%fused_computation.23 | convolution fusion | flops 1811939328 | bytes 8060928 | tf_op jit(solution)/shard_map/dot_general | solution.py:8
  149.3 0.0 copy-done.2
  149.3 6.2 %fusion.17 = f32[1152,384]{1,0:T(8,128)} fusion(bf16[1152,2048]{1,0:T(8,128)(2,1)} %bitcast.10, bf16[1,2048,384]{2,1,0:T(8,128)(2,1)S(1)} %copy-done.2), kind=kOutput, calls=%fused_computation.26 | convolution fusion | flops 1811939328 | bytes 8060928 | tf_op jit(solution)/shard_map/dot_general | solution.py:9
  155.4 91.8 %all-to-all-done = bf16[16,72,2048]{2,1,0:T(8,128)(2,1)} async-done(((bf16[16,72,2048]{2,1,0:T(8,128)(2,1)}), bf16[16,72,2048]{2,1,0:T(8,128)(2,1)}, u32[]{:S(2)}, u32[]{:S(2)}) %all-to-all-start) | async-done | bytes 4718624 | tf_op jit(solution)/shard_map/all_to_all | solution.py:53
  247.2 7.8 %fusion.21 = f32[2048,384]{1,0:T(8,128)} fusion(bf16[1152,2048]{1,0:T(8,128)(2,1)} %bitcast.6, f32[1152,384]{1,0:T(8,128)} %fusion.17, f32[1152,384]{1,0:T(8,128)} %fusion.14), kind=kOutput, calls=%fused_computation.30 | convolution fusion | flops 1814593536 | bytes 11403264 | tf_op jit(solution)/shard_map/dot_general | solution.py:22
  255.0 0.0 reduce-scatter.8.cloned.1.call-update
  255.1 0.3 reduce-scatter.4.cloned.1.call-start
  255.3 7.8 %multiply_convert_fusion.1 = (bf16[1152,384]{1,0:T(8,128)(2,1)}, bf16[1152,384]{1,0:T(8,128)(2,1)S(1)}) fusion(f32[1152,384]{1,0:T(8,128)} %fusion.14, f32[1152,384]{1,0:T(8,128)} %fusion.17, bf16[1152,2048]{1,0:T(8,128)(2,1)} %bitcast.6, bf16[1,2048,384]{2,1,0:T(8,128)(2,1)} %param.13), kind=kOutput, calls=%fused_computation.17 | convolution fusion | flops 1817690112 | bytes 11599872 | tf_op jit(solution)/shard_map/dot_general | solution.py:13
  263.2 0.0 copy-start.3
  263.2 0.9 copy-done.3
  264.1 7.0 %fusion.28 = f32[2048,384]{1,0:T(8,128)} fusion(bf16[1152,2048]{1,0:T(8,128)(2,1)} %bitcast.10, bf16[1152,384]{1,0:T(8,128)(2,1)S(1)} %get-tuple-element.5), kind=kOutput, calls=%fused_computation.43 | convolution fusion | flops 1811939328 | bytes 8749056 | tf_op jit(solution)/shard_map/dot_general | solution.py:20
  271.1 0.0 reduce-scatter.4.cloned.1.call-update
  271.1 0.0 copy-start.4
  271.1 3.9 fusion.12
  275.0 0.0 copy-done.4
  275.0 4.3 %fusion.1 = bf16[1152,2048]{1,0:T(8,128)(2,1)} fusion(f32[1152,2048]{1,0:T(8,128)S(1)} %fusion.12, bf16[1152,384]{1,0:T(8,128)(2,1)S(1)} %copy-done.4, bf16[1,2048,384]{2,1,0:T(8,128)(2,1)S(1)} %copy-done.2), kind=kOutput, calls=%fused_computation.6 | convolution fusion | flops 1816657920 | bytes 16613376 | tf_op jit(solution)/shard_map/dot_general | solution.py:19
  279.4 0.0 copy-start.5
  279.4 5.2 %all-to-all-start.2 = ((bf16[16,72,2048]{2,1,0:T(8,128)(2,1)}), bf16[16,72,2048]{2,1,0:T(8,128)(2,1)}, u32[]{:S(2)}, u32[]{:S(2)}) async-start(bf16[16,72,2048]{2,1,0:T(8,128)(2,1)} %bitcast.68), calls=%async_computation.2 | async-start | bytes 9437184 | tf_op jit(solution)/shard_map/all_to_all | solution.py:64
  284.6 0.3 reduce-scatter.6.cloned.1.call-start
  284.9 0.0 copy-done.5
  285.0 6.8 %fusion.29 = f32[2048,384]{1,0:T(8,128)} fusion(bf16[1152,2048]{1,0:T(8,128)(2,1)} %bitcast.10, bf16[1152,384]{1,0:T(8,128)(2,1)S(1)} %copy-done.5), kind=kOutput, calls=%fused_computation.44 | convolution fusion | flops 1811939328 | bytes 8749056 | tf_op jit(solution)/shard_map/dot_general | solution.py:21
  291.8 0.0 reduce-scatter.6.cloned.1.call-update
  291.8 97.3 %all-to-all-done.2 = bf16[16,72,2048]{2,1,0:T(8,128)(2,1)} async-done(((bf16[16,72,2048]{2,1,0:T(8,128)(2,1)}), bf16[16,72,2048]{2,1,0:T(8,128)(2,1)}, u32[]{:S(2)}, u32[]{:S(2)}) %all-to-all-start.2) | async-done | bytes 4718624 | tf_op jit(solution)/shard_map/all_to_all | solution.py:64
  389.1 0.0 copy-start.1
  389.1 11.9 %gather_fusion = bf16[1024,2048]{1,0:T(8,128)(2,1)} fusion(bf16[1152,2048]{1,0:T(8,128)(2,1)} %bitcast.14, s32[1024]{0:T(1024)S(1)} %broadcast_clamp_fusion), kind=kCustom, calls=%fused_computation | custom fusion | bytes 8392704 | tf_op jit(solution)/shard_map/gather | solution.py:72
  401.0 5.9 %bitcast_reduce_fusion = bf16[128,2048]{1,0:T(8,128)(2,1)} fusion(bf16[1024,2048]{1,0:T(8,128)(2,1)} %gather_fusion), kind=kLoop, calls=%fused_computation.8 | loop fusion | flops 1835008 | bytes 4718592 | tf_op jit(solution)/shard_map/reduce_sum | solution.py:73
  406.9 0.0 reduce-scatter.8.cloned.1.call-done
  406.9 0.0 reduce-scatter.4.cloned.1.call-done
  406.9 0.0 reduce-scatter.6.cloned.1.call-done
  406.9 0.0 copy-done.1
  (6 shorter events, 0.1 us)
Async XLA Ops:
  7.2 135.8 %copy-start = (bf16[1,2048,384]{2,1,0:T(8,128)(2,1)S(1)}, bf16[1,2048,384]{2,1,0:T(8,128)(2,1)}, u32[]{:S(2)}) copy-start(bf16[1,2048,384]{2,1,0:T(8,128)(2,1)} %param.11) | copy-start | bytes 4718596
  24.0 7.3 %copy-start.7 = (f32[128,8]{0,1:T(8,128)S(1)}, f32[128,8]{0,1:T(8,128)}, u32[]{:S(2)}) copy-start(f32[128,8]{0,1:T(8,128)} %param.9) | copy-start | bytes 12292
  24.0 7.5 %copy-start.6 = (bf16[128,2048]{1,0:T(8,128)(2,1)S(1)}, bf16[128,2048]{1,0:T(8,128)(2,1)}, u32[]{:S(2)}) copy-start(bf16[128,2048]{1,0:T(8,128)(2,1)} %param.10) | copy-start | bytes 1572868
  24.0 113.8 %all-to-all-start.1 = ((bf16[16,72,2048]{2,1,0:T(8,128)(2,1)}), bf16[16,72,2048]{2,1,0:T(8,128)(2,1)}, u32[]{:S(2)}, u32[]{:S(2)}) async-start(bf16[16,72,2048]{2,1,0:T(8,128)(2,1)} %bitcast.67), calls=%async_computation.1 | async-start | bytes 9437184 | tf_op jit(solution)/shard_map/all_to_all | solution.py:50
  137.8 109.4 %all-to-all-start = ((bf16[16,72,2048]{2,1,0:T(8,128)(2,1)}), bf16[16,72,2048]{2,1,0:T(8,128)(2,1)}, u32[]{:S(2)}, u32[]{:S(2)}) async-start(bf16[16,72,2048]{2,1,0:T(8,128)(2,1)} %bitcast.66), calls=%async_computation | async-start | bytes 9437184 | tf_op jit(solution)/shard_map/all_to_all | solution.py:53
  142.9 264.0 %reduce-scatter.8.cloned.1.call-start = ((), (), s32[]{:S(2)}) async-start(), calls=%async_computation.8 | async-start | bytes 4718592 | tf_op jit(solution)/shard_map/reduce_scatter | solution.py:77
  143.0 6.3 %copy-start.2 = (bf16[1,2048,384]{2,1,0:T(8,128)(2,1)S(1)}, bf16[1,2048,384]{2,1,0:T(8,128)(2,1)}, u32[]{:S(2)}) copy-start(bf16[1,2048,384]{2,1,0:T(8,128)(2,1)} %param.12) | copy-start | bytes 4718596
  255.1 151.8 %reduce-scatter.4.cloned.1.call-start = ((), (), s32[]{:S(2)}) async-start(), calls=%async_computation.6 | async-start | bytes 4718592 | tf_op jit(solution)/shard_map/reduce_scatter | solution.py:75
  263.2 0.9 copy-start.3
  271.1 3.9 copy-start.4
  279.4 5.6 %copy-start.5 = (bf16[1152,384]{1,0:T(8,128)(2,1)S(1)}, bf16[1152,384]{1,0:T(8,128)(2,1)}, u32[]{:S(2)}) copy-start(bf16[1152,384]{1,0:T(8,128)(2,1)} %get-tuple-element.4) | copy-start | bytes 2654212
  279.4 109.7 %all-to-all-start.2 = ((bf16[16,72,2048]{2,1,0:T(8,128)(2,1)}), bf16[16,72,2048]{2,1,0:T(8,128)(2,1)}, u32[]{:S(2)}, u32[]{:S(2)}) async-start(bf16[16,72,2048]{2,1,0:T(8,128)(2,1)} %bitcast.68), calls=%async_computation.2 | async-start | bytes 9437184 | tf_op jit(solution)/shard_map/all_to_all | solution.py:64
  284.6 122.3 %reduce-scatter.6.cloned.1.call-start = ((), (), s32[]{:S(2)}) async-start(), calls=%async_computation.7 | async-start | bytes 4718592 | tf_op jit(solution)/shard_map/reduce_scatter | solution.py:76
  389.1 17.8 %copy-start.1 = (bf16[1,2048,384]{2,1,0:T(8,128)(2,1)S(1)}, bf16[1,2048,384]{2,1,0:T(8,128)(2,1)}, u32[]{:S(2)}) copy-start(bf16[1,2048,384]{2,1,0:T(8,128)(2,1)} %param.11) | copy-start | bytes 4718596
Sparse Core Ops, SparseCore 0:
  255.2 10.1 reduce-scatter.7
  271.3 10.2 reduce-scatter.3
  291.9 12.0 reduce-scatter.5
where the time goes:
time: 414 us; the launch traced here: 413 us
  waiting for transfers between devices  286 us (69%)
  matrix products  50.2 us (12%)
  local copies, waits for them, and re-layouts  24.3 us (6%)
  other arithmetic  21.3 us (5%)
  starting transfers between devices  18.2 us (4%)
  between operations  13.9 us (3%)
    all_to_all x1, waiting for transfers between devices, on_device(): lax.all_to_all(back.reshape(experts, capacity, width), ('seq', 'exp'), sp...  97.3 us
    all_to_all x1, waiting for transfers between devices, on_device(): lax.all_to_all(send_x.reshape(shaped), ('seq', 'exp'), split_axis=0, conc...  96.4 us
    all_to_all x1, waiting for transfers between devices, on_device(): lax.all_to_all(send_dy.reshape(shaped), ('seq', 'exp'), split_axis=0, con...  91.8 us
    gather x1, local copies, waits for them, and re-layouts, on_device(): returned[target].reshape(tok_count, topk, width).astype(jnp.float32)  11.9 us
    scatter x1, other arithmetic, on_device(): jnp.zeros((experts * capacity, width), jnp.bfloat16).at[target].set(scaled)  9.83 us
    scatter x1, local copies, waits for them, and re-layouts, on_device(): jnp.zeros((experts * capacity, width), jnp.bfloat16).at[target].set(rows_x)  9.81 us
  transfers between devices with their start and end apart: 6, of which 3 were waited for; matrix products, arithmetic and copies ran while one was open for 17% of the time, Pallas kernels for 0%

commit v1 on v0

--- a/solution.py
+++ b/solution.py
@@ -1,7 +1,15 @@
+import functools
 import jax
 import jax.numpy as jnp
 from jax import lax
+from jax.experimental import pallas as pl
+from jax.experimental.pallas import tpu as pltpu
 from jax.sharding import PartitionSpec as P
+
+MESH = pl.DeviceIdType.MESH
+BF = jnp.bfloat16
+F32 = jnp.float32
+VMEM_BYTES = 62 * 1024 * 1024
 
 
 def expert_grads(x_rows, dy_rows, wg, wu, wd):
@@ -34,7 +42,9 @@
     capacity = pairs // experts + max(1, pairs // (8 * experts))
     flat_ids = route_ids.reshape(-1)
     onehot = (flat_ids[:, None] == jnp.arange(experts, dtype=jnp.int32)[None, :]).astype(jnp.int32)
-    earlier = jnp.cumsum(onehot, axis=0) - onehot
+    order = jnp.arange(pairs, dtype=jnp.int32)
+    lower = (order[:, None] > order[None, :]).astype(BF)
+    earlier = jnp.dot(lower, onehot.astype(BF), preferred_element_type=F32).astype(jnp.int32)
     slot_index = jnp.sum(earlier * onehot, axis=1)
     target = flat_ids * capacity + slot_index
     rows_x = jnp.broadcast_to(tokens[:, None, :], (tok_count, topk, width)).reshape(pairs, width)
@@ -79,6 +89,402 @@
     return (d_tokens, sum_g[None], sum_u[None], sum_d[None])
 
 
+def fused_kernel(
+    ns, ne, rows_half,
+    idt_ref, gt_ref, x_ref, d_ref, wg_hbm, wu_hbm, wd_hbm,
+    dt_ref, gg_ref, gu_ref, gd_ref,
+    meta_o, meta_i, xin, din, pall, gcol, cx, cd, rx, rd, wgu, wd,
+    ab, dh, dd, hid, bi, acc, po, pi, go, gi,
+    w_sem, zs, zr, es, er, bs, br, ps, pr, gs, gr,
+):
+    s = lax.axis_index("seq")
+    e = lax.axis_index("exp")
+    c = lax.axis_index("edp")
+    tok, width = x_ref.shape
+    hidn = wd.shape[1]
+    half_w = width // 2
+    topk = idt_ref.shape[0]
+    nch = ns // 2
+    rows = 2 * rows_half
+    allr = ne * rows
+    ct = min(512, width)
+
+    def plane(d):
+        return (lax.rem(s + d, ns), e, c)
+
+    def plane_back(d):
+        return (lax.rem(s + ns - d, ns), e, c)
+
+    def peer(j):
+        return (s, lax.rem(e + j, ne), c)
+
+    def peer_back(j):
+        return (s, lax.rem(e + ne - j, ne), c)
+
+    weights = [
+        pltpu.make_async_copy(wg_hbm, wgu.at[:, 0:hidn], w_sem.at[0]),
+        pltpu.make_async_copy(wu_hbm, wgu.at[:, hidn:2 * hidn], w_sem.at[1]),
+        pltpu.make_async_copy(wd_hbm, wd, w_sem.at[2]),
+    ]
+    for w in weights:
+        w.start()
+
+    barrier = pltpu.get_barrier_semaphore()
+    for d in range(1, ns):
+        pl.semaphore_signal(barrier, inc=1, device_id=plane(d), device_id_type=MESH)
+    for j in range(1, ne):
+        pl.semaphore_signal(barrier, inc=1, device_id=peer(j), device_id_type=MESH)
+    pl.semaphore_signal(barrier, inc=1, device_id=(s, e, 1 - c), device_id_type=MESH)
+
+    experts = ns * ne
+    ex = lax.broadcasted_iota(jnp.int32, (experts, tok), 0)
+    mask = jnp.zeros((experts, tok), F32)
+    gate = jnp.zeros((experts, tok), F32)
+    for k in range(topk):
+        eq = idt_ref[k:k + 1, :] == ex
+        mask = jnp.where(eq, 1.0, mask)
+        gate = jnp.where(eq, gt_ref[k:k + 1, :], gate)
+    before = (
+        lax.broadcasted_iota(jnp.int32, (tok, tok), 0)
+        < lax.broadcasted_iota(jnp.int32, (tok, tok), 1)
+    )
+    rank = jnp.dot(
+        mask.astype(BF), jnp.where(before, 1.0, 0.0).astype(BF), preferred_element_type=F32
+    )
+    slot = jnp.where(mask > 0.0, rank, -4096.0)
+    for z in range(ns):
+        meta_o[z, 0:ne, :] = slot[z * ne:(z + 1) * ne, :]
+        meta_o[z, ne:2 * ne, :] = gate[z * ne:(z + 1) * ne, :]
+    meta_i[0] = meta_o[s]
+
+    pl.semaphore_wait(barrier, ns - 1 + ne - 1 + 1)
+
+    def remote(src, dst, ss, rs, dev):
+        return pltpu.make_async_remote_copy(
+            src_ref=src, dst_ref=dst, send_sem=ss, recv_sem=rs, device_id=dev, device_id_type=MESH
+        )
+
+    mcp = [None] * ns
+    xcp = [None] * ns
+    dcp = [None] * ns
+    for d in range(1, ns):
+        mcp[d] = remote(
+            meta_o.at[lax.rem(s + d, ns)], meta_i.at[d], zs.at[0, d], zr.at[0, d], plane(d)
+        )
+        xcp[d] = remote(x_ref, xin.at[d], zs.at[1, d], zr.at[1, d], plane(d))
+        dcp[d] = remote(d_ref, din.at[d], zs.at[2, d], zr.at[2, d], plane(d))
+    xout = [[None] * ne for _ in range(nch)]
+    dout = [[None] * ne for _ in range(nch)]
+    bout = [[None] * ne for _ in range(nch)]
+    for k in range(nch):
+        for j in range(1, ne):
+            xout[k][j] = remote(cx.at[k, j], rx.at[k, j], es.at[0, k, j], er.at[0, k, j], peer(j))
+            dout[k][j] = remote(cd.at[k, j], rd.at[k, j], es.at[1, k, j], er.at[1, k, j], peer(j))
+            bout[k][j] = remote(cx.at[k, j], bi.at[k, j], bs.at[k, j], br.at[k, j], peer_back(j))
+    pout = [None] * ns
+    for d in range(1, ns):
+        pout[d] = remote(po.at[d], pi.at[d], ps.at[d], pr.at[d], plane_back(d))
+    partner = (s, e, 1 - c)
+    gout = [
+        remote(go.at[i], gi.at[i], gs.at[i], gr.at[i], partner) for i in range(3)
+    ]
+
+    def members(k):
+        return (k, k + nch)
+
+    def column(t, size):
+        return pl.ds(pl.multiple_of(t * size, size), size)
+
+    def make_select(k):
+        da_, db_ = members(k)
+        r = lax.broadcasted_iota(jnp.int32, (rows, 2 * tok), 0).astype(F32)
+        for j in range(ne):
+            idx = lax.rem(e + j, ne)
+            sl = jnp.concatenate(
+                [
+                    meta_i[da_, pl.ds(idx, 1), :],
+                    meta_i[db_, pl.ds(idx, 1), :] + float(rows_half),
+                ],
+                axis=1,
+            )
+            gl = jnp.concatenate(
+                [meta_i[da_, pl.ds(ne + idx, 1), :], meta_i[db_, pl.ds(ne + idx, 1), :]], axis=1
+            )
+            hit = r == sl
+            pall[k, j * rows:(j + 1) * rows, :] = jnp.where(hit, 1.0, 0.0).astype(BF)
+            g = jnp.sum(jnp.where(hit, gl, 0.0), axis=1, keepdims=True)
+            gcol[j * rows:(j + 1) * rows, :] = jnp.broadcast_to(g, (rows, 128))
+
+    def compact(k, own, arrived, out, got, scaled):
+        ra, rb = members(k)
+
+        def body(t, carry):
+            cs = column(t, ct)
+            first = own[:, cs] if ra == 0 else arrived[ra, :, cs]
+            both = jnp.concatenate([first, arrived[rb, :, cs]], axis=0)
+            y = jnp.dot(pall[k], both, preferred_element_type=F32)
+            if scaled:
+                y = y * gcol[:, 0:1]
+            y = y.astype(BF)
+            got[k, 0, :, cs] = y[0:rows]
+            for j in range(1, ne):
+                out[k, j, :, cs] = y[j * rows:(j + 1) * rows]
+            return carry
+
+        lax.fori_loop(0, width // ct, body, 0)
+
+    def gate_up(k):
+        for j in range(1, ne):
+            xout[k][j].wait_recv()
+
+        def body(t, carry):
+            cs = column(t, 256)
+            ab[:, cs] = jnp.dot(
+                rx[k].reshape(allr, width), wgu[:, cs], preferred_element_type=F32
+            )
+            return carry
+
+        lax.fori_loop(0, 2 * hidn // 256, body, 0)
+
+    def middle(k):
+        for j in range(1, ne):
+            dout[k][j].wait_recv()
+        dh[...] = jnp.dot(rd[k].reshape(allr, width), wd[...], preferred_element_type=F32)
+
+        def act_body(t, carry):
+            rs_ = pl.ds(pl.multiple_of(t * 16, 16), 16)
+            a = ab[rs_, 0:hidn]
+            b = ab[rs_, hidn:2 * hidn]
+            g = dh[rs_, :]
+            sig = jax.nn.sigmoid(a)
+            act = a * sig
+            hid[rs_, :] = (act * b).astype(BF)
+            dd[rs_, 0:hidn] = (g * b * sig * (1.0 + a * (1.0 - sig))).astype(BF)
+            dd[rs_, hidn:2 * hidn] = (g * act).astype(BF)
+            return carry
+
+        lax.fori_loop(0, allr // 16, act_body, 0)
+        for j in range(1, ne):
+            xout[k][j].wait_send()
+
+        def back_body(t, carry):
+            cs = column(t, ct)
+            y = lax.dot_general(
+                dd[...], wgu[cs, :], (((1,), (1,)), ((), ())), preferred_element_type=F32
+            ).astype(BF)
+            bi[k, 0, :, cs] = y[0:rows]
+            for j in range(1, ne):
+                cx[k, j, :, cs] = y[j * rows:(j + 1) * rows]
+            return carry
+
+        lax.fori_loop(0, width // ct, back_body, 0)
+        for j in range(1, ne):
+            bout[k][j].start()
+
+    zero = (((0,), (0,)), ((), ()))
+
+    def grads(k, half, outs):
+        gt = min(256, half_w)
+
+        def body(t, carry):
+            cs = pl.ds(pl.multiple_of(half * half_w + t * gt, gt), gt)
+            rs_ = column(t, gt)
+            xt = rx[k, :, :, cs].reshape(allr, gt)
+            dt = rd[k, :, :, cs].reshape(allr, gt)
+            xg = lax.dot_general(xt, dd[...], zero, preferred_element_type=F32)
+            dg = lax.dot_general(dt, hid[...], zero, preferred_element_type=F32)
+            if k == 0:
+                outs[0][rs_, :] = xg[:, 0:hidn]
+                outs[1][rs_, :] = xg[:, hidn:2 * hidn]
+                outs[2][rs_, :] = dg
+            else:
+                outs[0][rs_, :] += xg[:, 0:hidn]
+                outs[1][rs_, :] += xg[:, hidn:2 * hidn]
+                outs[2][rs_, :] += dg
+            return carry
+
+        lax.fori_loop(0, half_w // gt, body, 0)
+
+    def combine(k):
+        for j in range(1, ne):
+            bout[k][j].wait_recv()
+        ra, rb = members(k)
+
+        def body(t, carry):
+            cs = column(t, ct)
+            y = lax.dot_general(
+                pall[k], bi[k, :, :, cs].reshape(allr, ct), zero, preferred_element_type=F32
+            )
+            if ra == 0:
+                acc[:, cs] = y[0:tok]
+            else:
+                po[ra, :, cs] = y[0:tok].astype(BF)
+            po[rb, :, cs] = y[tok:2 * tok].astype(BF)
+            return carry
+
+        lax.fori_loop(0, width // ct, body, 0)
+        for d in (ra, rb):
+            if d:
+                pout[d].start()
+
+    def arrive(copies, k):
+        for d in members(k):
+            if d:
+                copies[d].wait_recv()
+
+    def depart(copies, k):
+        for d in members(k):
+            if d:
+                copies[d].start()
+
+    for d in range(1, ns):
+        mcp[d].start()
+    depart(xcp, 0)
+    arrive(mcp, 0)
+    make_select(0)
+    for k in range(nch):
+        if k:
+            arrive(mcp, k)
+            make_select(k)
+        arrive(xcp, k)
+        if k == 0:
+            depart(dcp, 0)
+            if nch > 1:
+                depart(xcp, 1)
+        compact(k, x_ref, xin, cx, rx, False)
+        for j in range(1, ne):
+            xout[k][j].start()
+        if k:
+            middle(k - 1)
+        arrive(dcp, k)
+        if k + 1 < nch:
+            depart(dcp, k + 1)
+        if k and k + 1 < nch:
+            depart(xcp, k + 1)
+        compact(k, d_ref, din, cd, rd, True)
+        for j in range(1, ne):
+            dout[k][j].start()
+        if k == 0:
+            for w in weights:
+                w.wait()
+        else:
+            grads(k - 1, 1 - c, (go.at[0], go.at[1], go.at[2]))
+            grads(k - 1, c, (gg_ref, gu_ref, gd_ref))
+            combine(k - 1)
+        gate_up(k)
+    last = nch - 1
+    middle(last)
+    grads(last, 1 - c, (go.at[0], go.at[1], go.at[2]))
+    for g in gout:
+        g.start()
+    grads(last, c, (gg_ref, gu_ref, gd_ref))
+    combine(last)
+    for g in gout:
+        g.wait_recv()
+    gg_ref[...] += gi[0]
+    gu_ref[...] += gi[1]
+    gd_ref[...] += gi[2]
+    for d in range(1, ns):
+        pout[d].wait_recv()
+
+    def final(t, carry):
+        cs = column(t, ct)
+        y = acc[:, cs]
+        for d in range(1, ns):
+            y = y + pi[d, :, cs].astype(F32)
+        dt_ref[:, cs] = y.astype(BF)
+        return carry
+
+    lax.fori_loop(0, width // ct, final, 0)
+    for d in range(1, ns):
+        mcp[d].wait_send()
+        xcp[d].wait_send()
+        dcp[d].wait_send()
+        pout[d].wait_send()
+    for k in range(nch):
+        for j in range(1, ne):
+            dout[k][j].wait_send()
+            bout[k][j].wait_send()
+    for g in gout:
+        g.wait_send()
+
+
+def sizes(ns, ne, tok, topk, width, hidn):
+    experts = ns * ne
+    capacity = tok * topk // experts + max(1, tok * topk // (8 * experts))
+    rows_half = -(-capacity // 8) * 8
+    rows = 2 * rows_half
+    nch = max(1, ns // 2)
+    allr = ne * rows
+    scratch = [
+        ((ns, 2 * ne, tok), F32),
+        ((ns, 2 * ne, tok), F32),
+        ((ns, tok, width), BF),
+        ((ns, tok, width), BF),
+        ((nch, allr, 2 * tok), BF),
+        ((allr, 128), F32),
+        ((nch, ne, rows, width), BF),
+        ((nch, ne, rows, width), BF),
+        ((nch, ne, rows, width), BF),
+        ((nch, ne, rows, width), BF),
+        ((width, 2 * hidn), BF),
+        ((width, hidn), BF),
+        ((allr, 2 * hidn), F32),
+        ((allr, hidn), F32),
+        ((allr, 2 * hidn), BF),
+        ((allr, hidn), BF),
+        ((nch, ne, rows, width), BF),
+        ((tok, width), F32),
+        ((ns, tok, width), BF),
+        ((ns, tok, width), BF),
+        ((3, width // 2, hidn), F32),
+        ((3, width // 2, hidn), F32),
+    ]
+    total = 0
+    for shape, kind in scratch:
+        n = 1
+        for v in shape:
+            n *= v
+        total += n * jnp.dtype(kind).itemsize
+    total += 3 * (width // 2) * hidn * 4 + 3 * tok * width * 2
+    return rows_half, nch, scratch, total
+
+
+def fused(tokens, route_ids, gates, d_out, w_gate, w_up, w_down):
+    ns = lax.axis_size("seq")
+    ne = lax.axis_size("exp")
+    tok, width = tokens.shape
+    topk = route_ids.shape[1]
+    hidn = w_gate.shape[2]
+    rows_half, nch, scratch, _ = sizes(ns, ne, tok, topk, width, hidn)
+    dma = pltpu.SemaphoreType.DMA
+    vm = pl.BlockSpec(memory_space=pltpu.VMEM)
+    hbm = pl.BlockSpec(memory_space=pl.ANY)
+    half = jax.ShapeDtypeStruct((width // 2, hidn), F32)
+    pairs = tok * ns * topk * 9 // 8
+    out = pl.pallas_call(
+        functools.partial(fused_kernel, ns, ne, rows_half),
+        out_shape=(jax.ShapeDtypeStruct((tok, width), BF), half, half, half),
+        in_specs=[vm, vm, vm, vm, hbm, hbm, hbm],
+        out_specs=(vm, vm, vm, vm),
+        scratch_shapes=[pltpu.VMEM(sh, kind) for sh, kind in scratch] + [
+            dma((3,)),
+            dma((3, ns)), dma((3, ns)),
+            dma((2, nch, ne)), dma((2, nch, ne)),
+            dma((nch, ne)), dma((nch, ne)),
+            dma((ns,)), dma((ns,)),
+            dma((3,)), dma((3,)),
+        ],
+        compiler_params=pltpu.CompilerParams(
+            collective_id=0, has_side_effects=True, vmem_limit_bytes=VMEM_BYTES
+        ),
+        cost_estimate=pl.CostEstimate(
+            flops=16 * pairs * width * hidn, bytes_accessed=12 * width * hidn, transcendentals=0
+        ),
+    )(route_ids.T, gates.T, tokens, d_out, w_gate[0], w_up[0], w_down[0])
+    return (out[0], out[1][None], out[2][None], out[3][None])
+
+
 def solution(mesh):
     in_specs = (
         P(("seq", "exp", "edp"), None),
@@ -95,6 +501,18 @@
         P(("seq", "exp"), "edp", None),
         P(("seq", "exp"), "edp", None),
     )
-    return jax.shard_map(
-        on_device, mesh=mesh, in_specs=in_specs, out_specs=out_specs, check_vma=False
-    )
+    def shard(body):
+        return jax.shard_map(
+            body, mesh=mesh, in_specs=in_specs, out_specs=out_specs, check_vma=False
+        )
+
+    ns, ne, nd = mesh.shape["seq"], mesh.shape["exp"], mesh.shape["edp"]
+
+    def whole(tokens, route_ids, gates, d_out, w_gate, w_up, w_down):
+        tok = tokens.shape[0] // (ns * ne * nd)
+        total = sizes(ns, ne, tok, route_ids.shape[1], tokens.shape[1], w_gate.shape[2])[3]
+        fits = total < VMEM_BYTES - 3 * 1024 * 1024
+        body = fused if fits and ns % 2 == 0 and nd == 2 and tok % 128 == 0 else on_device
+        return shard(body)(tokens, route_ids, gates, d_out, w_gate, w_up, w_down)
+
+    return whole

time: 414 us -> 235 us (0.57)
  waiting for transfers between devices: 286 us -> 0 us
  Pallas kernels: 0 us -> 225 us
  matrix products: 50.2 us -> 0 us
  other arithmetic: 21.3 us -> 0 us
  starting transfers between devices: 18.2 us -> 0 us
  local copies, waits for them, and re-layouts: 24.3 us -> 7.77 us
  between operations: 13.9 us -> 0.64 us
    all_to_all x3 -> x0, waiting for transfers between devices: 285 us -> none  [the longest x1 97.3 us: on_device(): lax.all_to_all(back.reshape(experts, capacity, width), ('seq', 'exp'), sp...]
    pallas_call x0 -> x1, Pallas kernels: none -> 225 us  [fused(): pl.pallas_call(functools.partial(fused_kernel, ns, ne, rows_half), out_sh...]
    dot_general x8 -> x0, matrix products: 50.2 us -> none  [the longest x1 7.85 us: expert_grads(): d_hidden = jnp.dot(dy_rows, wd, preferred_element_type=jnp.float32)]
    all_to_all x3 -> x0, starting transfers between devices: 17.6 us -> none  [the longest x1 7.27 us: on_device(): lax.all_to_all(send_x.reshape(shaped), ('seq', 'exp'), split_axis=0, conc...]
    gather x1 -> x0, local copies, waits for them, and re-layouts: 11.9 us -> none  [on_device(): returned[target].reshape(tok_count, topk, width).astype(jnp.float32)]
    scatter x1 -> x0, other arithmetic: 9.83 us -> none  [on_device(): jnp.zeros((experts * capacity, width), jnp.bfloat16).at[target].set(scaled)]
    scatter x1 -> x0, local copies, waits for them, and re-layouts: 9.81 us -> none  [on_device(): jnp.zeros((experts * capacity, width), jnp.bfloat16).at[target].set(rows_x)]
    unnamed x18 -> x8, local copies, waits for them, and re-layouts: 1.85 us -> 7.77 us
  transfers between devices with their start and end apart: 6 -> 0, of which waited for: 3 -> 0; matrix products, arithmetic and copies ran while one was open for 17% -> 0% of each run, Pallas kernels for 0% -> 0%
where the time goes in v1:
time: 235 us; the launch traced here: 233 us
  Pallas kernels  225 us (96%)
  local copies, waits for them, and re-layouts  7.77 us (3%)
    pallas_call x1, Pallas kernels, fused(): pl.pallas_call(functools.partial(fused_kernel, ns, ne, rows_half), out_sh...  225 us
    unnamed x8, local copies, waits for them, and re-layouts  7.77 us

profile of v1, /device:TPU:14, one launch (start us, length us, event | category | flops | bytes accessed | tf_op | source)
XLA Modules:
  0.0 233.4 jit_solution(13304473655068934581)
XLA Ops:
  0.6 225.0 %shard_map.102 = (bf16[128,2048]{1,0:T(8,128)(2,1)}, f32[1024,384]{1,0:T(8,128)}, f32[1024,384]{1,0:T(8,128)}, f32[1024,384]{1,0:T(8,128)}) custom-call(s32[8,128]{1,0:T(8,128)} %bitcast.14, f32[8,128]{1,0:T(8,128)} %bitcast.15, bf16[128,2048]{1,0:T(8,128)(2,1)} %x_ref.1, bf16[128,2048]{1,0:T(8,128)(2,1)} %d_ref.1, bf16[2048,384]{1,0:T(8,128)(2,1)} %bitcast.11, ...), custom_call_target="tpu_custom_call" | custom-call | flops 57982058496 | bytes 9437184 | tf_op jit(solution)/shard_map/pallas_call | solution.py:465
  225.7 1.9 copy.15
  227.6 0.0 copy-start.1
  227.6 2.8 %copy.16 = f32[1,1024,384]{2,1,0:T(8,128)} copy(f32[1,1024,384]{2,1,0:T(8,128)} %bitcast.10) | data formatting | bytes 3145728
  230.3 0.0 copy-done.1
  230.3 0.0 copy-start
  230.3 1.1 copy.17
  231.5 0.8 copy-done
  232.3 1.1 copy.18
Async XLA Ops:
  227.6 2.8 %copy-start.1 = (f32[1024,384]{1,0:T(8,128)S(1)}, f32[1024,384]{1,0:T(8,128)}, u32[]{:S(2)}) copy-start(f32[1024,384]{1,0:T(8,128)} %get-tuple-element.10) | copy-start | bytes 4718596
  230.3 2.0 copy-start

commit v2 on v1

--- a/solution.py
+++ b/solution.py
@@ -10,6 +10,7 @@
 BF = jnp.bfloat16
 F32 = jnp.float32
 VMEM_BYTES = 62 * 1024 * 1024
+PARTS = 4
 
 
 def expert_grads(x_rows, dy_rows, wg, wu, wd):
@@ -89,13 +90,17 @@
     return (d_tokens, sum_g[None], sum_u[None], sum_d[None])
 
 
+def far_first(ne):
+    return range(ne - 1, 0, -1)
+
+
 def fused_kernel(
     ns, ne, rows_half,
     idt_ref, gt_ref, x_ref, d_ref, wg_hbm, wu_hbm, wd_hbm,
     dt_ref, gg_ref, gu_ref, gd_ref,
     meta_o, meta_i, xin, din, pall, gcol, cx, cd, rx, rd, wgu, wd,
     ab, dh, dd, hid, bi, acc, po, pi, go, gi,
-    w_sem, zs, zr, es, er, bs, br, ps, pr, gs, gr,
+    w_sem, ms, zs, zr, es, er, bs, br, ps, pr, gs, gr,
 ):
     s = lax.axis_index("seq")
     e = lax.axis_index("exp")
@@ -107,7 +112,13 @@
     nch = ns // 2
     rows = 2 * rows_half
     allr = ne * rows
-    ct = min(512, width)
+    parts = PARTS
+    pw = width // parts
+    ct = min(512, pw)
+    per = pw // ct
+
+    def span(q):
+        return slice(q * pw, (q + 1) * pw)
 
     def plane(d):
         return (lax.rem(s + d, ns), e, c)
@@ -115,11 +126,15 @@
     def plane_back(d):
         return (lax.rem(s + ns - d, ns), e, c)
 
+    def peer_index(j):
+        total, bit = 0, 1
+        while bit < ne:
+            total = total + lax.rem(e // bit + j // bit, 2) * bit
+            bit *= 2
+        return total
+
     def peer(j):
-        return (s, lax.rem(e + j, ne), c)
-
-    def peer_back(j):
-        return (s, lax.rem(e + ne - j, ne), c)
+        return (s, peer_index(j), c)
 
     weights = [
         pltpu.make_async_copy(wg_hbm, wgu.at[:, 0:hidn], w_sem.at[0]),
@@ -164,26 +179,47 @@
             src_ref=src, dst_ref=dst, send_sem=ss, recv_sem=rs, device_id=dev, device_id_type=MESH
         )
 
-    mcp = [None] * ns
-    xcp = [None] * ns
-    dcp = [None] * ns
+    def grid(*dims):
+        if not dims:
+            return None
+        return [grid(*dims[1:]) for _ in range(dims[0])]
+
+    mcp = grid(ns)
+    xcp = grid(ns, parts)
+    dcp = grid(ns, parts)
+    pout = grid(ns, parts)
     for d in range(1, ns):
         mcp[d] = remote(
-            meta_o.at[lax.rem(s + d, ns)], meta_i.at[d], zs.at[0, d], zr.at[0, d], plane(d)
+            meta_o.at[lax.rem(s + d, ns)], meta_i.at[d], ms.at[0, d], ms.at[1, d], plane(d)
         )
-        xcp[d] = remote(x_ref, xin.at[d], zs.at[1, d], zr.at[1, d], plane(d))
-        dcp[d] = remote(d_ref, din.at[d], zs.at[2, d], zr.at[2, d], plane(d))
-    xout = [[None] * ne for _ in range(nch)]
-    dout = [[None] * ne for _ in range(nch)]
-    bout = [[None] * ne for _ in range(nch)]
+        for q in range(parts):
+            cs = span(q)
+            xcp[d][q] = remote(
+                x_ref.at[:, cs], xin.at[d, :, cs], zs.at[0, d, q], zr.at[0, d, q], plane(d)
+            )
+            dcp[d][q] = remote(
+                d_ref.at[:, cs], din.at[d, :, cs], zs.at[1, d, q], zr.at[1, d, q], plane(d)
+            )
+            pout[d][q] = remote(
+                po.at[d, :, cs], pi.at[d, :, cs], ps.at[d, q], pr.at[d, q], plane_back(d)
+            )
+    xout = grid(nch, parts, ne)
+    dout = grid(nch, parts, ne)
+    bout = grid(nch, parts, ne)
     for k in range(nch):
-        for j in range(1, ne):
-            xout[k][j] = remote(cx.at[k, j], rx.at[k, j], es.at[0, k, j], er.at[0, k, j], peer(j))
-            dout[k][j] = remote(cd.at[k, j], rd.at[k, j], es.at[1, k, j], er.at[1, k, j], peer(j))
-            bout[k][j] = remote(cx.at[k, j], bi.at[k, j], bs.at[k, j], br.at[k, j], peer_back(j))
-    pout = [None] * ns
-    for d in range(1, ns):
-        pout[d] = remote(po.at[d], pi.at[d], ps.at[d], pr.at[d], plane_back(d))
+        for q in range(parts):
+            cs = span(q)
+            for j in range(1, ne):
+                at = (k, j, slice(None), cs)
+                xout[k][q][j] = remote(
+                    cx.at[at], rx.at[at], es.at[0, k, q, j], er.at[0, k, q, j], peer(j)
+                )
+                dout[k][q][j] = remote(
+                    cd.at[at], rd.at[at], es.at[1, k, q, j], er.at[1, k, q, j], peer(j)
+                )
+                bout[k][q][j] = remote(
+                    cx.at[at], bi.at[at], bs.at[k, q, j], br.at[k, q, j], peer(j)
+                )
     partner = (s, e, 1 - c)
     gout = [
         remote(go.at[i], gi.at[i], gs.at[i], gr.at[i], partner) for i in range(3)
@@ -199,7 +235,7 @@
         da_, db_ = members(k)
         r = lax.broadcasted_iota(jnp.int32, (rows, 2 * tok), 0).astype(F32)
         for j in range(ne):
-            idx = lax.rem(e + j, ne)
+            idx = peer_index(j)
             sl = jnp.concatenate(
                 [
                     meta_i[da_, pl.ds(idx, 1), :],
@@ -215,7 +251,7 @@
             g = jnp.sum(jnp.where(hit, gl, 0.0), axis=1, keepdims=True)
             gcol[j * rows:(j + 1) * rows, :] = jnp.broadcast_to(g, (rows, 128))
 
-    def compact(k, own, arrived, out, got, scaled):
+    def compact(k, q, own, arrived, out, got, scaled):
         ra, rb = members(k)
 
         def body(t, carry):
@@ -231,11 +267,12 @@
                 out[k, j, :, cs] = y[j * rows:(j + 1) * rows]
             return carry
 
-        lax.fori_loop(0, width // ct, body, 0)
+        lax.fori_loop(q * per, (q + 1) * per, body, 0)
 
     def gate_up(k):
-        for j in range(1, ne):
-            xout[k][j].wait_recv()
+        for q in range(parts):
+            for j in range(1, ne):
+                xout[k][q][j].wait_recv()
 
         def body(t, carry):
             cs = column(t, 256)
@@ -247,8 +284,9 @@
         lax.fori_loop(0, 2 * hidn // 256, body, 0)
 
     def middle(k):
-        for j in range(1, ne):
-            dout[k][j].wait_recv()
+        for q in range(parts):
+            for j in range(1, ne):
+                dout[k][q][j].wait_recv()
         dh[...] = jnp.dot(rd[k].reshape(allr, width), wd[...], preferred_element_type=F32)
 
         def act_body(t, carry):
@@ -264,8 +302,9 @@
             return carry
 
         lax.fori_loop(0, allr // 16, act_body, 0)
-        for j in range(1, ne):
-            xout[k][j].wait_send()
+        for q in range(parts):
+            for j in range(1, ne):
+                xout[k][q][j].wait_send()
 
         def back_body(t, carry):
             cs = column(t, ct)
@@ -277,9 +316,10 @@
                 cx[k, j, :, cs] = y[j * rows:(j + 1) * rows]
             return carry
 
-        lax.fori_loop(0, width // ct, back_body, 0)
-        for j in range(1, ne):
-            bout[k][j].start()
+        for q in range(parts):
+            lax.fori_loop(q * per, (q + 1) * per, back_body, 0)
+            for j in far_first(ne):
+                bout[k][q][j].start()
 
     zero = (((0,), (0,)), ((), ()))
 
@@ -306,8 +346,6 @@
         lax.fori_loop(0, half_w // gt, body, 0)
 
     def combine(k):
-        for j in range(1, ne):
-            bout[k][j].wait_recv()
         ra, rb = members(k)
 
         def body(t, carry):
@@ -322,48 +360,55 @@
             po[rb, :, cs] = y[tok:2 * tok].astype(BF)
             return carry
 
-        lax.fori_loop(0, width // ct, body, 0)
-        for d in (ra, rb):
-            if d:
-                pout[d].start()
-
-    def arrive(copies, k):
+        for q in range(parts):
+            for j in range(1, ne):
+                bout[k][q][j].wait_recv()
+            lax.fori_loop(q * per, (q + 1) * per, body, 0)
+            for d in (rb, ra):
+                if d:
+                    pout[d][q].start()
+
+    def arrive(copies, k, q):
         for d in members(k):
             if d:
-                copies[d].wait_recv()
+                copies[d][q].wait_recv()
 
     def depart(copies, k):
+        for q in range(parts):
+            for d in members(k):
+                if d:
+                    copies[d][q].start()
+
+    def arrive_meta(k):
         for d in members(k):
             if d:
-                copies[d].start()
+                mcp[d].wait_recv()
 
     for d in range(1, ns):
         mcp[d].start()
     depart(xcp, 0)
-    arrive(mcp, 0)
+    depart(dcp, 0)
+    arrive_meta(0)
     make_select(0)
     for k in range(nch):
         if k:
-            arrive(mcp, k)
+            arrive_meta(k)
             make_select(k)
-        arrive(xcp, k)
-        if k == 0:
-            depart(dcp, 0)
-            if nch > 1:
-                depart(xcp, 1)
-        compact(k, x_ref, xin, cx, rx, False)
-        for j in range(1, ne):
-            xout[k][j].start()
+        for q in range(parts):
+            arrive(xcp, k, q)
+            compact(k, q, x_ref, xin, cx, rx, False)
+            for j in far_first(ne):
+                xout[k][q][j].start()
+        if k + 1 < nch:
+            depart(xcp, k + 1)
+            depart(dcp, k + 1)
         if k:
             middle(k - 1)
-        arrive(dcp, k)
-        if k + 1 < nch:
-            depart(dcp, k + 1)
-        if k and k + 1 < nch:
-            depart(xcp, k + 1)
-        compact(k, d_ref, din, cd, rd, True)
-        for j in range(1, ne):
-            dout[k][j].start()
+        for q in range(parts):
+            arrive(dcp, k, q)
+            compact(k, q, d_ref, din, cd, rd, True)
+            for j in far_first(ne):
+                dout[k][q][j].start()
         if k == 0:
             for w in weights:
                 w.wait()
@@ -384,8 +429,6 @@
     gg_ref[...] += gi[0]
     gu_ref[...] += gi[1]
     gd_ref[...] += gi[2]
-    for d in range(1, ns):
-        pout[d].wait_recv()
 
     def final(t, carry):
         cs = column(t, ct)
@@ -395,16 +438,21 @@
         dt_ref[:, cs] = y.astype(BF)
         return carry
 
-    lax.fori_loop(0, width // ct, final, 0)
+    for q in range(parts):
+        for d in range(1, ns):
+            pout[d][q].wait_recv()
+        lax.fori_loop(q * per, (q + 1) * per, final, 0)
     for d in range(1, ns):
         mcp[d].wait_send()
-        xcp[d].wait_send()
-        dcp[d].wait_send()
-        pout[d].wait_send()
+        for q in range(parts):
+            xcp[d][q].wait_send()
+            dcp[d][q].wait_send()
+            pout[d][q].wait_send()
     for k in range(nch):
-        for j in range(1, ne):
-            dout[k][j].wait_send()
-            bout[k][j].wait_send()
+        for q in range(parts):
+            for j in range(1, ne):
+                dout[k][q][j].wait_send()
+                bout[k][q][j].wait_send()
     for g in gout:
         g.wait_send()
 
@@ -469,10 +517,11 @@
         out_specs=(vm, vm, vm, vm),
         scratch_shapes=[pltpu.VMEM(sh, kind) for sh, kind in scratch] + [
             dma((3,)),
-            dma((3, ns)), dma((3, ns)),
-            dma((2, nch, ne)), dma((2, nch, ne)),
-            dma((nch, ne)), dma((nch, ne)),
-            dma((ns,)), dma((ns,)),
+            dma((2, ns)),
+            dma((2, ns, PARTS)), dma((2, ns, PARTS)),
+            dma((2, nch, PARTS, ne)), dma((2, nch, PARTS, ne)),
+            dma((nch, PARTS, ne)), dma((nch, PARTS, ne)),
+            dma((ns, PARTS)), dma((ns, PARTS)),
             dma((3,)), dma((3,)),
         ],
         compiler_params=pltpu.CompilerParams(
@@ -512,7 +561,7 @@
         tok = tokens.shape[0] // (ns * ne * nd)
         total = sizes(ns, ne, tok, route_ids.shape[1], tokens.shape[1], w_gate.shape[2])[3]
         fits = total < VMEM_BYTES - 3 * 1024 * 1024
-        body = fused if fits and ns % 2 == 0 and nd == 2 and tok % 128 == 0 else on_device
+        body = fused if fits and ns % 2 == 0 and nd == 2 and ne & (ne - 1) == 0 and tok % 128 == 0 else on_device
         return shard(body)(tokens, route_ids, gates, d_out, w_gate, w_up, w_down)
 
     return whole

time: 235 us -> 211 us (0.90)
  Pallas kernels: 225 us -> 199 us
    pallas_call x1, Pallas kernels: 225 us -> 199 us  [fused(): pl.pallas_call(functools.partial(fused_kernel, ns, ne, rows_half), out_sh...]
where the time goes in v2:
time: 211 us; the launch traced here: 207 us
  Pallas kernels  199 us (94%)
  local copies, waits for them, and re-layouts  7.77 us (4%)
    pallas_call x1, Pallas kernels, fused(): pl.pallas_call(functools.partial(fused_kernel, ns, ne, rows_half), out_sh...  199 us
    unnamed x8, local copies, waits for them, and re-layouts  7.77 us

profile of v2, /device:TPU:14, one launch (start us, length us, event | category | flops | bytes accessed | tf_op | source)
XLA Modules:
  0.0 207.1 jit_solution(13719719032863711536)
XLA Ops:
  0.6 198.7 %shard_map.102 = (bf16[128,2048]{1,0:T(8,128)(2,1)}, f32[1024,384]{1,0:T(8,128)}, f32[1024,384]{1,0:T(8,128)}, f32[1024,384]{1,0:T(8,128)}) custom-call(s32[8,128]{1,0:T(8,128)} %bitcast.14, f32[8,128]{1,0:T(8,128)} %bitcast.15, bf16[128,2048]{1,0:T(8,128)(2,1)} %x_ref.1, bf16[128,2048]{1,0:T(8,128)(2,1)} %d_ref.1, bf16[2048,384]{1,0:T(8,128)(2,1)} %bitcast.11, ...), custom_call_target="tpu_custom_call" | custom-call | flops 57982058496 | bytes 9437184 | tf_op jit(solution)/shard_map/pallas_call | solution.py:513
  199.4 1.9 copy.15
  201.2 0.0 copy-start.1
  201.2 2.8 %copy.16 = f32[1,1024,384]{2,1,0:T(8,128)} copy(f32[1,1024,384]{2,1,0:T(8,128)} %bitcast.10) | data formatting | bytes 3145728
  204.0 0.0 copy-done.1
  204.0 0.0 copy-start
  204.0 1.1 copy.17
  205.2 0.8 copy-done
  206.0 1.1 copy.18
Async XLA Ops:
  201.2 2.8 %copy-start.1 = (f32[1024,384]{1,0:T(8,128)S(1)}, f32[1024,384]{1,0:T(8,128)}, u32[]{:S(2)}) copy-start(f32[1024,384]{1,0:T(8,128)} %get-tuple-element.10) | copy-start | bytes 4718596
  204.0 2.0 copy-start
